TPU v7x, 512 devices: a whole 4x8x8 slice. The times are simulated.
512 devices in a mesh: leaf: 4 (over x), row: 16 (over z, core), col: 8 (over y).
Axes of the slice: x: 4, y: 8, z: 8, core: 2. Of those that a mesh axis runs over, the one named last changes fastest.
Arguments:
- widths: int32 [15], replicated, may hold values from 1024 to 2048, as said below
- bottom_lists: int32 [8, 32], P('leaf'), may hold values from 0 to 47, as said below
- root_inverse: bfloat16 [2048, 2048], P('row')
- second_panels: bfloat16 [4, 2048, 1024], P('leaf', 'row', 'col'), may hold values from -0.09375 to 0.09375
- second_inverse: bfloat16 [4, 1024, 2048], P('leaf', 'col', 'row')
- third_panels: bfloat16 [4, 2, 2048, 2048], P('leaf', None, 'row', 'col'), may hold values from -0.09375 to 0.09375
- third_inverse: bfloat16 [4, 2048, 2048], P('leaf', 'col', 'row')
- bottom_panels: bfloat16 [8, 4096, 2048], P('leaf', 'row', 'col'), may hold values from -0.09375 to 0.09375
- bottom_inverse: bfloat16 [8, 2048, 2048], P('leaf', 'col', 'row')
Outputs:
- second_off: bfloat16 [4, 2048, 1024], P('leaf', 'row', 'col')
- second_diag: bfloat16 [4, 1024, 2048], P('leaf', 'col', 'row')
- third_off: bfloat16 [4, 2, 2048, 2048], P('leaf', None, 'row', 'col')
- third_diag: bfloat16 [4, 2048, 2048], P('leaf', 'col', 'row')
- bottom_off: bfloat16 [8, 3, 2048, 2048], P('leaf', None, 'row', 'col')
- bottom_diag: bfloat16 [8, 2048, 2048], P('leaf', 'col', 'row')
Inputs may be any that keep to these rules, and one draw needn't show every extreme that they name: `widths`: some supernode has 2048 columns and some 2048/2. `bottom_lists`: row e lists 32 different blocks of 128 rows of its chain (root, then second-level ancestor, then parent, 16 blocks each) in increasing order; block 0 and all blocks of the parent are always listed.
All inputs are finite; a program needn't handle non-finite values.
Results may differ from a plain program's by a relative error of at most 0.015.
Values may be sent and summed in bfloat16 or wider, within the bound.
A program may use at most 64 MiB of HBM per device.

v0:
```python
import jax
import jax.numpy as jnp
from jax import lax
from jax.sharding import PartitionSpec as P

NODES = 15
BOTTOM = 8


def partner(block, axis, apart):
    count = lax.axis_size(axis)
    route = []
    for low in range(count):
        high = low | 1 << apart
        if high != low and high < count:
            route += [(low, high), (high, low)]
    return lax.ppermute(block, axis, route)


def node_width(widths, node_at):
    return jnp.sum(jnp.where(jnp.arange(widths.shape[0]) == node_at, widths, 0))


def chain_fold(flat_chain, tile_width, ancestors, shard_piece):
    piece_rows = shard_piece.shape[1]
    picked = jnp.concatenate(
        [
            lax.dynamic_slice_in_dim(flat_chain, level_at * tile_width, piece_rows, 1)
            for level_at in range(ancestors)
        ],
        axis=1,
    )
    stacked = shard_piece.reshape(ancestors * piece_rows, shard_piece.shape[2])
    return jnp.dot(picked, stacked, preferred_element_type=jnp.float32)


def local(
    widths,
    bottom_lists,
    root_inverse,
    second_panels,
    second_inverse,
    third_panels,
    third_inverse,
    bottom_panels,
    bottom_inverse,
):
    group_at = lax.axis_index("leaf")
    row_at = lax.axis_index("row")
    col_at = lax.axis_index("col")
    rows_dev = root_inverse.shape[0]
    tile_width = root_inverse.shape[1]
    half_cols = second_panels.shape[2]
    own_cols = third_panels.shape[3]
    half_at = group_at % 2
    parent_one = 1 + group_at // 2
    node_two = 3 + group_at
    row_first = row_at * rows_dev
    row_index = row_first + jnp.arange(rows_dev)
    root_width = node_width(widths, 0)
    root_mask = (row_index < root_width)[:, None] & (jnp.arange(tile_width) < root_width)[None, :]
    root_block = jnp.where(root_mask, root_inverse, 0)
    width_one = node_width(widths, parent_one)
    mask_rows_one = row_index < width_one
    first_col = half_at * (tile_width // 2) + col_at * half_cols
    mask_cols_one = first_col + jnp.arange(half_cols) < width_one
    panel_one = jnp.where(mask_cols_one[None, :], second_panels[0], 0)
    flat_piece = lax.all_gather(panel_one, "row", axis=0, tiled=True)
    product_one = jnp.dot(root_block, flat_piece, preferred_element_type=jnp.float32)
    off_one = (-product_one).astype(jnp.bfloat16)
    mine_half = lax.all_gather(off_one, "col", axis=1, tiled=True)
    other_half = partner(mine_half, "leaf", 0)
    off_full = jnp.where(
        half_at == 0,
        jnp.concatenate([mine_half, other_half], 1),
        jnp.concatenate([other_half, mine_half], 1),
    )
    term_one = lax.dot_general(
        panel_one, off_full, (((0,), (0,)), ((), ())), preferred_element_type=jnp.float32
    )
    summed_one = lax.psum_scatter(
        term_one.astype(jnp.bfloat16), "row", scatter_dimension=1, tiled=True
    ).astype(jnp.float32)
    inverse_one = jnp.where(
        mask_cols_one[:, None] & mask_rows_one[None, :], second_inverse[0], 0
    ).astype(jnp.float32)
    diag_one = (inverse_one - summed_one).astype(jnp.bfloat16)
    mine_diag = lax.all_gather(diag_one.T, "col", axis=1, tiled=True)
    other_diag = partner(mine_diag, "leaf", 0)
    diag_full = jnp.where(
        half_at == 0,
        jnp.concatenate([mine_diag, other_diag], 1),
        jnp.concatenate([other_diag, mine_diag], 1),
    )
    second_off = off_one[None]
    second_diag = diag_one[None]
    turned_one = lax.all_to_all(off_full, "row", split_axis=1, concat_axis=0, tiled=True)
    chain_two = jnp.stack(
        [jnp.concatenate([root_block, off_full], 1), jnp.concatenate([turned_one.T, diag_full], 1)],
        0,
    )
    flat_two = chain_two.reshape(2 * rows_dev, 2 * tile_width)
    first_own = col_at * own_cols
    width_two = node_width(widths, node_two)
    mask_cols_two = first_own + jnp.arange(own_cols) < width_two
    panel_two = jnp.where(mask_cols_two[None, None, :], third_panels[0], 0)
    product_two = chain_fold(
        flat_two, tile_width, 2, lax.all_gather(panel_two, "row", axis=1, tiled=True)
    )
    off_two = (-product_two).astype(jnp.bfloat16).reshape(2, rows_dev, own_cols)
    full_two = lax.all_gather(off_two, "col", axis=2, tiled=True)
    term_two = jnp.einsum("kin,kim->nm", panel_two, full_two, preferred_element_type=jnp.float32)
    summed_two = lax.psum_scatter(
        term_two.astype(jnp.bfloat16), "row", scatter_dimension=1, tiled=True
    ).astype(jnp.float32)
    mask_rows_two = row_index < width_two
    inverse_two = jnp.where(
        mask_cols_two[:, None] & mask_rows_two[None, :], third_inverse[0], 0
    ).astype(jnp.float32)
    diag_two = (inverse_two - summed_two).astype(jnp.bfloat16)
    diag_rows_two = lax.all_gather(diag_two.T, "col", axis=1, tiled=True)
    turned_two = lax.all_to_all(full_two, "row", split_axis=2, concat_axis=1, tiled=True)
    lower_two = jnp.transpose(turned_two, (2, 0, 1)).reshape(rows_dev, 2 * tile_width)
    chain_three = jnp.stack(
        [
            jnp.concatenate([chain_two[0], full_two[0]], 1),
            jnp.concatenate([chain_two[1], full_two[1]], 1),
            jnp.concatenate([lower_two, diag_rows_two], 1),
        ],
        0,
    )
    flat_three = chain_three.reshape(3 * rows_dev, 3 * tile_width)
    bottom_dev = bottom_panels.shape[0]
    list_len = bottom_lists.shape[1]
    block_rows = 2 * tile_width // list_len
    node_three = NODES - BOTTOM + bottom_dev * group_at + jnp.arange(bottom_dev)
    width_three = jnp.sum(
        jnp.where(jnp.arange(widths.shape[0])[None, :] == node_three[:, None], widths[None, :], 0),
        1,
    )
    mask_cols_three = (first_own + jnp.arange(own_cols))[None, :] < width_three[:, None]
    panel_three = jnp.where(mask_cols_three[:, None, :], bottom_panels, 0)
    positions = (
        jnp.repeat(bottom_lists, block_rows, axis=1) * block_rows
        + jnp.arange(list_len * block_rows) % block_rows
    )
    own_chain = (jnp.arange(3)[:, None] * tile_width + row_index[None, :]).reshape(-1)
    matches = bottom_lists[:, :, None] == (own_chain // block_rows)[None, None, :]
    member = jnp.any(matches, axis=1)
    lower_all = lax.all_gather(panel_three, "row", axis=1, tiled=True)
    spread = jax.vmap(
        lambda where_to, values_in: jnp.zeros((3 * tile_width, own_cols), jnp.bfloat16)
        .at[where_to]
        .set(values_in)
    )(positions, lower_all)
    product_three = jnp.einsum(
        "ab,ebn->ean", flat_three, spread, preferred_element_type=jnp.float32
    )
    chain_rows = lax.dynamic_slice_in_dim(
        spread.reshape(bottom_dev, 3, tile_width, own_cols), row_first, rows_dev, 2
    )
    off_three = jnp.where(member[:, :, None], -product_three, 0.0).astype(jnp.bfloat16)
    off_three = off_three.reshape(bottom_dev, 3, rows_dev, own_cols)
    full_three = lax.all_gather(off_three, "col", axis=3, tiled=True)
    term_three = jnp.einsum(
        "ekin,ekim->enm", chain_rows, full_three, preferred_element_type=jnp.float32
    )
    summed_three = lax.psum_scatter(
        term_three.astype(jnp.bfloat16), "row", scatter_dimension=2, tiled=True
    ).astype(jnp.float32)
    mask_rows_three = row_index[None, :] < width_three[:, None]
    inverse_three = jnp.where(
        mask_cols_three[:, :, None] & mask_rows_three[:, None, :], bottom_inverse, 0
    ).astype(jnp.float32)
    diag_three = (inverse_three - summed_three).astype(jnp.bfloat16)
    return (second_off, second_diag, off_two[None], diag_two[None], off_three, diag_three)


def solution(mesh):
    in_specs = (
        P(),
        P("leaf", None),
        P("row", None),
        P("leaf", "row", "col"),
        P("leaf", "col", "row"),
        P("leaf", None, "row", "col"),
        P("leaf", "col", "row"),
        P("leaf", "row", "col"),
        P("leaf", "col", "row"),
    )
    out_specs = (
        P("leaf", "row", "col"),
        P("leaf", "col", "row"),
        P("leaf", None, "row", "col"),
        P("leaf", "col", "row"),
        P("leaf", None, "row", "col"),
        P("leaf", "col", "row"),
    )
    return jax.shard_map(local, mesh=mesh, in_specs=in_specs, out_specs=out_specs, check_vma=False)
```

profile of v0, /device:TPU:8, one launch (start us, length us, event | category | flops | bytes accessed | tf_op | source)
XLA Modules:
  0.0 519.0 jit_solution(5305973732029650270)
XLA Ops:
  8.1 1.3 fusion.20
  10.2 24.6 %all_gather.24 = bf16[2048,128]{0,1:T(8,128)(2,1)S(1)} all-gather(bf16[128,128]{0,1:T(8,128)(2,1)S(1)} %bitcast_select_fusion.1), channel_id=1, replica_groups=mesh['leaf'=4,'row'=16,'col'=8] {'row'}, dimensions={0}, use_global_device_ids=true | all-gather | bytes 557056 | tf_op jit(solution)/shard_map/all_gather | solution.py:68
  36.1 1.3 and_select_fusion
  37.7 23.5 %all_gather.25 = bf16[128,1024]{1,0:T(8,128)(2,1)S(1)} all-gather(bf16[128,128]{1,0:T(8,128)(2,1)S(1)} %fusion.7), channel_id=1, replica_groups=mesh['leaf'=4,'row'=16,'col'=8] {'col'}, dimensions={1}, use_global_device_ids=true | all-gather | bytes 294912 | tf_op jit(solution)/shard_map/all_gather | solution.py:71
  61.3 3.5 collective-permute-start
  64.8 4.9 collective-permute-done
  73.4 3.6 all-to-all-start
  77.8 49.9 %reduce-scatter.6.cloned.1.call-done = bf16[128,128]{0,1:T(8,128)(2,1)} async-done(((bf16[128,2048]{0,1:T(8,128)(2,1)}), bf16[128,128]{0,1:T(8,128)(2,1)}) %reduce-scatter.6.cloned.1.call-update) | async-done | bytes 32784 | tf_op jit(solution)/shard_map/reduce_scatter | solution.py:81
  128.6 23.1 %all_gather.26 = bf16[128,1024]{1,0:T(8,128)(2,1)S(1)} all-gather(bf16[128,128]{1,0:T(8,128)(2,1)S(1)} %get-tuple-element.37), channel_id=1, replica_groups=mesh['leaf'=4,'row'=16,'col'=8] {'col'}, dimensions={1}, use_global_device_ids=true | all-gather | bytes 294912 | tf_op jit(solution)/shard_map/all_gather | solution.py:88
  151.7 3.2 collective-permute-start.1
  155.2 4.8 collective-permute-done.1
  161.3 1.5 pad_maximum_fusion.1
  162.8 9.9 %all-gather.5.cloned.1.call-done = bf16[2,2048,256]{2,1,0:T(8,128)(2,1)} async-done(((bf16[2,128,256]{2,1,0:T(8,128)(2,1)}), bf16[2,2048,256]{2,1,0:T(8,128)(2,1)}) %all-gather.5.cloned.1.call-update) | async-done | bytes 2097168 | tf_op jit(solution)/shard_map/all_gather | solution.py:108
  172.8 3.6 fusion.6
  176.5 39.9 %all-gather.7.cloned.1.call-done = bf16[2,128,2048]{2,1,0:T(8,128)(2,1)} async-done(((bf16[2,128,256]{2,1,0:T(8,128)(2,1)}), bf16[2,128,2048]{2,1,0:T(8,128)(2,1)}) %all-gather.7.cloned.1.call-update) | async-done | bytes 1048592 | tf_op jit(solution)/shard_map/all_gather | solution.py:111
  216.4 2.8 fusion.2
  220.8 2.0 copy.69
  222.8 7.5 %all-to-all-start.1 = ((bf16[2,128,2048]{1,0,2:T(2,128)(2,1)}), bf16[2,128,2048]{1,0,2:T(2,128)(2,1)}, u32[]{:S(2)}, u32[]{:S(2)}) async-start(bf16[2,128,2048]{1,0,2:T(2,128)(2,1)} %copy.69), calls=%async_computation.3 | async-start | bytes 2097152 | tf_op jit(solution)/shard_map/all_to_all | solution.py:122
  231.5 2.3 maximum_bitcast_fusion
  233.8 24.9 %all-to-all-done.1 = bf16[2,128,2048]{1,0,2:T(2,128)(2,1)} async-done(((bf16[2,128,2048]{1,0,2:T(2,128)(2,1)}), bf16[2,128,2048]{1,0,2:T(2,128)(2,1)}, u32[]{:S(2)}, u32[]{:S(2)}) %all-to-all-start.1) | async-done | bytes 1048608 | tf_op jit(solution)/shard_map/all_to_all | solution.py:122
  258.8 1.9 copy.95
  261.1 25.3 %reduce-scatter.8.cloned.1.call-done = bf16[256,128]{0,1:T(8,128)(2,1)} async-done(((bf16[256,2048]{0,1:T(8,128)(2,1)}), bf16[256,128]{0,1:T(8,128)(2,1)}) %reduce-scatter.8.cloned.1.call-update) | async-done | bytes 65552 | tf_op jit(solution)/shard_map/reduce_scatter | solution.py:113
  287.3 25.9 %all_gather.30 = bf16[128,2048]{1,0:T(8,128)(2,1)S(1)} all-gather(bf16[128,256]{1,0:T(8,128)(2,1)S(1)} %get-tuple-element.35), channel_id=1, replica_groups=mesh['leaf'=4,'row'=16,'col'=8] {'col'}, dimensions={1}, use_global_device_ids=true | all-gather | bytes 589824 | tf_op jit(solution)/shard_map/all_gather | solution.py:121
  313.3 3.6 pad_maximum_fusion
  317.0 18.1 %all-gather.9.cloned.1.call-done = bf16[2,4096,256]{2,1,0:T(8,128)(2,1)} async-done(((bf16[2,256,256]{2,1,0:T(8,128)(2,1)}), bf16[2,4096,256]{2,1,0:T(8,128)(2,1)}) %all-gather.9.cloned.1.call-update) | async-done | bytes 4194320 | tf_op jit(solution)/shard_map/all_gather | solution.py:150
  335.1 39.1 %scatter_custom_fusion = bf16[12288,256]{1,0:T(8,128)(2,1)} fusion(s32[8192]{0:T(1024)S(1)} %bitcast.140, bf16[8192,256]{1,0:T(8,128)(2,1)} %bitcast.141, bf16[]{:T(256)} %constant.73.clone.1), kind=kCustom, calls=%fused_computation.3 | custom fusion | bytes 6291968
  374.1 7.6 %fusion.5 = bf16[2,384,256]{1,2,0:T(8,128)(2,1)S(1)} fusion(bf16[2,6144,256]{2,1,0:T(8,128)(2,1)} %bitcast.125, bf16[384,6144,1]{1,0,2:T(8,128)(2,1)} %bitcast.127, pred[2,384]{1,0:T(4,128)(4,1)S(1)} %compare_reduce_fusion), kind=kOutput, calls=%fused_computation.15 | convolution fusion | flops 2416508928 | bytes 11404032 | tf_op jit(solution)/shard_map/ab,ebn->ean/dot_general | solution.py:156
  382.7 57.5 %all-gather.11.cloned.1.call-done = bf16[2,3,128,2048]{3,2,1,0:T(8,128)(2,1)} async-done(((bf16[2,3,128,256]{3,2,1,0:T(8,128)(2,1)}), bf16[2,3,128,2048]{3,2,1,0:T(8,128)(2,1)}) %all-gather.11.cloned.1.call-update) | async-done | bytes 3145744 | tf_op jit(solution)/shard_map/all_gather | solution.py:164
  440.2 3.3 bitcast_convert_fusion
  443.6 3.8 copy.83
  447.4 3.4 copy.91
  452.3 57.9 %reduce-scatter.10.cloned.1.call-done = bf16[128,512]{1,0:T(8,128)(2,1)} async-done(((bf16[2048,512]{1,0:T(8,128)(2,1)}), bf16[128,512]{1,0:T(8,128)(2,1)}) %reduce-scatter.10.cloned.1.call-update) | async-done | bytes 131088
  (93 shorter events, 18.6 us)
Async XLA Ops:
  7.2 64.5 %copy-start.5 = (bf16[1,2,128,256]{3,2,1,0:T(8,128)(2,1)S(1)}, bf16[1,2,128,256]{3,2,1,0:T(8,128)(2,1)}, u32[]{:S(2)}) copy-start(bf16[1,2,128,256]{3,2,1,0:T(8,128)(2,1)} %param.14) | copy-start | bytes 393220
  7.2 120.6 %reduce-scatter.6.cloned.1.call-start = ((), (), s32[]{:S(2)}) async-start(), calls=%async_computation.5 | async-start | bytes 557056 | tf_op jit(solution)/shard_map/reduce_scatter | solution.py:81
  37.7 35.7 %copy-start.4 = (bf16[128,128]{1,0:T(8,128)(2,1)}, bf16[128,128]{1,0:T(8,128)(2,1)S(1)}, u32[]{:S(2)}) copy-start(bf16[128,128]{1,0:T(8,128)(2,1)S(1)} %fusion.7) | copy-start | bytes 98308
  61.3 15.8 %copy-start.8 = (bf16[1,128,128]{2,1,0:T(8,128)(2,1)S(1)}, bf16[1,128,128]{2,1,0:T(8,128)(2,1)}, u32[]{:S(2)}) copy-start(bf16[1,128,128]{2,1,0:T(8,128)(2,1)} %param.13) | copy-start | bytes 98308
  61.3 8.4 %collective-permute-start = (bf16[128,1024]{1,0:T(8,128)(2,1)S(1)}, bf16[128,1024]{1,0:T(8,128)(2,1)S(1)}, u32[]{:S(2)}, u32[]{:S(2)}) collective-permute-start(bf16[128,1024]{1,0:T(8,128)(2,1)S(1)} %all_gather.25), channel_id=1, source_target_pairs={{0,128},{128,0},{256,384},{384,256},{1,129},{129,1},{257,385},{385... | collective-permute-start | bytes 786440 | tf_op jit(solution)/shard_map/ppermute | solution.py:17
  71.0 101.8 %all-gather.5.cloned.1.call-start = ((), (), s32[]{:S(2)}) async-start(), calls=%async_computation.6 | async-start | bytes 2228224 | tf_op jit(solution)/shard_map/all_gather | solution.py:108
  73.4 81.6 %all-to-all-start = ((bf16[128,16,128]{2,0,1:T(8,128)(2,1)}), bf16[128,16,128]{2,0,1:T(8,128)(2,1)S(1)}, u32[]{:S(2)}, u32[]{:S(2)}) async-start(bf16[128,16,128]{2,0,1:T(8,128)(2,1)} %maximum_select_fusion.1), calls=%async_computation.1 | async-start | bytes 1048576 | tf_op jit(solution)/shard_map/all_to_all | solution.py:97
  77.0 139.4 %all-gather.7.cloned.1.call-start = ((), (), s32[]{:S(2)}) async-start(), calls=%async_computation.7 | async-start | bytes 1179648 | tf_op jit(solution)/shard_map/all_gather | solution.py:111
  151.7 8.4 %collective-permute-start.1 = (bf16[128,1024]{1,0:T(8,128)(2,1)S(1)}, bf16[128,1024]{1,0:T(8,128)(2,1)}, u32[]{:S(2)}, u32[]{:S(2)}) collective-permute-start(bf16[128,1024]{1,0:T(8,128)(2,1)S(1)} %all_gather.26), channel_id=1, source_target_pairs={{0,128},{128,0},{256,384},{384,256},{1,129},{129,1},{257,385},{385... | collective-permute-start | bytes 786440 | tf_op jit(solution)/shard_map/ppermute | solution.py:17
  161.2 1.6 copy-start.1
  162.8 53.6 %copy-start.2 = (bf16[2,128,256]{2,1,0:T(8,128)(2,1)S(1)}, bf16[2,128,256]{2,1,0:T(8,128)(2,1)}, u32[]{:S(2)}) copy-start(bf16[2,128,256]{2,1,0:T(8,128)(2,1)} %bitcast_select_fusion) | copy-start | bytes 393220
  172.8 46.6 %copy-start.12 = (s32[15]{0:T(128)S(1)}, s32[15]{0:T(128)}, u32[]{:S(2)}) copy-start(s32[15]{0:T(128)} %param.9) | copy-start | bytes 184
  172.8 46.9 %copy-start.3 = (bf16[2,256,256]{2,1,0:T(8,128)(2,1)S(1)}, bf16[2,256,256]{2,1,0:T(8,128)(2,1)}, u32[]{:S(2)}) copy-start(bf16[2,256,256]{2,1,0:T(8,128)(2,1)} %param.16) | copy-start | bytes 786436
  176.4 44.0 %copy-start.9 = (s32[2,32]{1,0:T(2,128)S(1)}, s32[2,32]{1,0:T(2,128)}, u32[]{:S(2)}) copy-start(s32[2,32]{1,0:T(2,128)} %param.10) | copy-start | bytes 772
  176.4 44.2 %copy-start.11 = (s32[2]{0:T(128)S(1)}, s32[2]{0:T(128)}, u32[]{:S(2)}) copy-start(s32[2]{0:T(128)} %constant.94) | copy-start | bytes 28
  176.4 44.3 %copy-start.10 = (s32[2]{0:T(128)S(1)}, s32[2]{0:T(128)}, u32[]{:S(2)}) copy-start(s32[2]{0:T(128)} %constant.97) | copy-start | bytes 28
  176.4 110.0 %reduce-scatter.8.cloned.1.call-start = ((), (), s32[]{:S(2)}) async-start(), calls=%async_computation.8 | async-start | bytes 1114112 | tf_op jit(solution)/shard_map/reduce_scatter | solution.py:113
  216.4 4.4 copy-start
  219.2 11.2 %copy-start.7 = (bf16[1,256,128]{2,1,0:T(8,128)(2,1)S(1)}, bf16[1,256,128]{2,1,0:T(8,128)(2,1)}, u32[]{:S(2)}) copy-start(bf16[1,256,128]{2,1,0:T(8,128)(2,1)} %param.15) | copy-start | bytes 196612
  219.3 115.8 %all-gather.9.cloned.1.call-start = ((), (), s32[]{:S(2)}) async-start(), calls=%async_computation.9 | async-start | bytes 4456448 | tf_op jit(solution)/shard_map/all_gather | solution.py:150
  222.8 35.9 %all-to-all-start.1 = ((bf16[2,128,2048]{1,0,2:T(2,128)(2,1)}), bf16[2,128,2048]{1,0,2:T(2,128)(2,1)}, u32[]{:S(2)}, u32[]{:S(2)}) async-start(bf16[2,128,2048]{1,0,2:T(2,128)(2,1)} %copy.69), calls=%async_computation.3 | async-start | bytes 2097152 | tf_op jit(solution)/shard_map/all_to_all | solution.py:122
  230.4 209.9 %all-gather.11.cloned.1.call-start = ((), (), s32[]{:S(2)}) async-start(), calls=%async_computation.10 | async-start | bytes 3538944 | tf_op jit(solution)/shard_map/all_gather | solution.py:164
  382.7 127.6 %reduce-scatter.10.cloned.1.call-start = ((), (), s32[]{:S(2)}) async-start(), calls=%async_computation.11 | async-start | bytes 2228224
  447.4 64.0 %copy-start.6 = (bf16[2,256,128]{2,1,0:T(8,128)(2,1)S(1)}, bf16[2,256,128]{2,1,0:T(8,128)(2,1)}, u32[]{:S(2)}) copy-start(bf16[2,256,128]{2,1,0:T(8,128)(2,1)} %param.17) | copy-start | bytes 393220
Sparse Core Ops, SparseCore 0:
  71.1 56.6 reduce-scatter.5
  130.7 42.0 all-gather.4
  176.5 39.8 all-gather.6
  219.4 66.9 reduce-scatter.7
  288.9 46.0 all-gather.8
  382.8 57.3 all-gather.10
  450.9 59.3 reduce-scatter.9
where the time goes:
time: 520 us; the launch traced here: 519 us
  waiting for transfers between devices  293 us (56%)
  blocking collectives  97.1 us (19%)
  local copies, waits for them, and re-layouts  55.7 us (11%)
  other arithmetic  21.3 us (4%)
  matrix products  18.9 us (4%)
  starting transfers between devices  18.1 us (3%)
  between operations  14.6 us (3%)
    unnamed x8, waiting for transfers between devices  58.1 us
    all_gather x1, waiting for transfers between devices, local(): full_three = lax.all_gather(off_three, 'col', axis=3, tiled=True)  57.5 us
    unnamed x39, local copies, waits for them, and re-layouts  50.3 us
    reduce_scatter x1, waiting for transfers between devices, local(): lax.psum_scatter(term_one.astype(jnp.bfloat16), 'row', scatter_dimension=...  49.9 us
    all_gather x1, waiting for transfers between devices, local(): full_two = lax.all_gather(off_two, 'col', axis=2, tiled=True)  39.9 us
    all_gather x1, blocking collectives, local(): diag_rows_two = lax.all_gather(diag_two.T, 'col', axis=1, tiled=True)  25.9 us
    reduce_scatter x1, waiting for transfers between devices, local(): lax.psum_scatter(term_two.astype(jnp.bfloat16), 'row', scatter_dimension=...  25.3 us
    all_to_all x1, waiting for transfers between devices, local(): lax.all_to_all(full_two, 'row', split_axis=2, concat_axis=1, tiled=True)  24.9 us
  transfers between devices with their start and end apart: 11, of which 10 were waited for; matrix products, arithmetic and copies ran while one was open for 4% of the time, Pallas kernels for 0%

commit v1 on v0

--- a/solution.py
+++ b/solution.py
@@ -119,7 +119,19 @@
     ).astype(jnp.float32)
     diag_two = (inverse_two - summed_two).astype(jnp.bfloat16)
     diag_rows_two = lax.all_gather(diag_two.T, "col", axis=1, tiled=True)
-    turned_two = lax.all_to_all(full_two, "row", split_axis=2, concat_axis=1, tiled=True)
+
+    def _move_thing(vector, mesh_ax, axis_no, array_dim):
+        return jnp.concatenate(
+            lax.all_to_all(
+                jnp.stack(jnp.split(vector, lax.psum(1, mesh_ax), axis=axis_no), axis=0),
+                mesh_ax,
+                0,
+                0,
+            ),
+            array_dim,
+        )
+
+    turned_two = _move_thing(full_two, "row", 2, 1)
     lower_two = jnp.transpose(turned_two, (2, 0, 1)).reshape(rows_dev, 2 * tile_width)
     chain_three = jnp.stack(
         [

time: 520 us -> 523 us (level)
  the two profiles are of different devices: /device:TPU:8 before, /device:TPU:2 now
where the time goes in v1:
time: 523 us; the launch traced here: 522 us
  waiting for transfers between devices  282 us (54%)
  blocking collectives  101 us (19%)
  local copies, waits for them, and re-layouts  66.1 us (13%)
  other arithmetic  22.4 us (4%)
  matrix products  18.9 us (4%)
  starting transfers between devices  16.5 us (3%)
  between operations  14.6 us (3%)
    unnamed x8, waiting for transfers between devices  60.1 us
    unnamed x53, local copies, waits for them, and re-layouts  59.5 us
    all_gather x1, waiting for transfers between devices, local(): full_three = lax.all_gather(off_three, 'col', axis=3, tiled=True)  55.5 us
    reduce_scatter x1, waiting for transfers between devices, local(): lax.psum_scatter(term_one.astype(jnp.bfloat16), 'row', scatter_dimension=...  48.9 us
    all_gather x1, waiting for transfers between devices, local(): full_two = lax.all_gather(off_two, 'col', axis=2, tiled=True)  39.9 us
    all_gather x1, blocking collectives, local(): diag_rows_two = lax.all_gather(diag_two.T, 'col', axis=1, tiled=True)  27.5 us
    all_to_all x1, waiting for transfers between devices, _move_thing(): lax.all_to_all(jnp.stack(jnp.split(vector, lax.psum(1, mesh_ax), axis=axi...  25.5 us
    all_gather x1, blocking collectives, local(): mine_half = lax.all_gather(off_one, 'col', axis=1, tiled=True)  25 us
  transfers between devices with their start and end apart: 11, of which 10 were waited for; matrix products, arithmetic and copies ran while one was open for 6% of the time, Pallas kernels for 0%

profile of v1, /device:TPU:2, one launch (start us, length us, event | category | flops | bytes accessed | tf_op | source)
XLA Modules:
  0.0 521.7 jit_solution(13412036987379010157)
XLA Ops:
  8.1 1.3 fusion.36
  10.2 24.6 %all_gather.24 = bf16[2048,128]{0,1:T(8,128)(2,1)S(1)} all-gather(bf16[128,128]{0,1:T(8,128)(2,1)S(1)} %bitcast_select_fusion.1), channel_id=1, replica_groups=mesh['leaf'=4,'row'=16,'col'=8] {'row'}, dimensions={0}, use_global_device_ids=true | all-gather | bytes 557056 | tf_op jit(solution)/shard_map/all_gather | solution.py:68
  37.7 25.0 %all_gather.25 = bf16[128,1024]{1,0:T(8,128)(2,1)S(1)} all-gather(bf16[128,128]{1,0:T(8,128)(2,1)S(1)} %fusion.7), channel_id=1, replica_groups=mesh['leaf'=4,'row'=16,'col'=8] {'col'}, dimensions={1}, use_global_device_ids=true | all-gather | bytes 294912 | tf_op jit(solution)/shard_map/all_gather | solution.py:71
  62.7 2.6 collective-permute-start
  65.3 5.8 %collective-permute-done = bf16[128,1024]{1,0:T(8,128)(2,1)S(1)} collective-permute-done((bf16[128,1024]{1,0:T(8,128)(2,1)S(1)}, bf16[128,1024]{1,0:T(8,128)(2,1)S(1)}, u32[]{:S(2)}, u32[]{:S(2)}) %collective-permute-start) | collective-permute-done | bytes 262176 | tf_op jit(solution)/shard_map/ppermute | solution.py:17
  74.8 3.6 all-to-all-start
  79.2 48.9 %reduce-scatter.6.cloned.1.call-done = bf16[128,128]{0,1:T(8,128)(2,1)} async-done(((bf16[128,2048]{0,1:T(8,128)(2,1)}), bf16[128,128]{0,1:T(8,128)(2,1)}) %reduce-scatter.6.cloned.1.call-update) | async-done | bytes 32784 | tf_op jit(solution)/shard_map/reduce_scatter | solution.py:81
  129.0 24.0 %all_gather.26 = bf16[128,1024]{1,0:T(8,128)(2,1)S(1)} all-gather(bf16[128,128]{1,0:T(8,128)(2,1)S(1)} %get-tuple-element.37), channel_id=1, replica_groups=mesh['leaf'=4,'row'=16,'col'=8] {'col'}, dimensions={1}, use_global_device_ids=true | all-gather | bytes 294912 | tf_op jit(solution)/shard_map/all_gather | solution.py:88
  153.0 2.6 collective-permute-start.1
  155.9 5.5 %collective-permute-done.1 = bf16[128,1024]{1,0:T(8,128)(2,1)} collective-permute-done((bf16[128,1024]{1,0:T(8,128)(2,1)S(1)}, bf16[128,1024]{1,0:T(8,128)(2,1)}, u32[]{:S(2)}, u32[]{:S(2)}) %collective-permute-start.1) | collective-permute-done | bytes 262176 | tf_op jit(solution)/shard_map/ppermute | solution.py:17
  162.6 1.5 pad_maximum_fusion.1
  164.1 8.7 %all-gather.5.cloned.1.call-done = bf16[2,2048,256]{2,1,0:T(8,128)(2,1)} async-done(((bf16[2,128,256]{2,1,0:T(8,128)(2,1)}), bf16[2,2048,256]{2,1,0:T(8,128)(2,1)}) %all-gather.5.cloned.1.call-update) | async-done | bytes 2097168 | tf_op jit(solution)/shard_map/all_gather | solution.py:108
  172.8 3.6 fusion.6
  176.5 39.9 %all-gather.7.cloned.1.call-done = bf16[2,128,2048]{2,1,0:T(8,128)(2,1)} async-done(((bf16[2,128,256]{2,1,0:T(8,128)(2,1)}), bf16[2,128,2048]{2,1,0:T(8,128)(2,1)}) %all-gather.7.cloned.1.call-update) | async-done | bytes 1048592 | tf_op jit(solution)/shard_map/all_gather | solution.py:111
  216.5 2.8 fusion.2
  231.1 7.5 %all-to-all-start.1 = ((bf16[16,2,128,128]{3,2,1,0:T(8,128)(2,1)}), bf16[16,2,128,128]{3,2,1,0:T(8,128)(2,1)}, u32[]{:S(2)}, u32[]{:S(2)}) async-start(bf16[16,2,128,128]{3,2,1,0:T(8,128)(2,1)} %fusion.9), calls=%async_computation.3 | async-start | bytes 2097152 | tf_op jit(solution)/shard_map/all_to_all | solution.py:125
  239.8 2.3 maximum_bitcast_fusion
  242.1 25.5 %all-to-all-done.1 = bf16[16,2,128,128]{3,2,1,0:T(8,128)(2,1)} async-done(((bf16[16,2,128,128]{3,2,1,0:T(8,128)(2,1)}), bf16[16,2,128,128]{3,2,1,0:T(8,128)(2,1)}, u32[]{:S(2)}, u32[]{:S(2)}) %all-to-all-start.1) | async-done | bytes 1048608 | tf_op jit(solution)/shard_map/all_to_all | solution.py:125
  267.5 2.3 copy.69
  269.9 2.3 copy.83
  272.1 15.0 %reduce-scatter.8.cloned.1.call-done = bf16[256,128]{0,1:T(8,128)(2,1)} async-done(((bf16[256,2048]{0,1:T(8,128)(2,1)}), bf16[256,128]{0,1:T(8,128)(2,1)}) %reduce-scatter.8.cloned.1.call-update) | async-done | bytes 65552 | tf_op jit(solution)/shard_map/reduce_scatter | solution.py:113
  288.1 27.5 %all_gather.30 = bf16[128,2048]{1,0:T(8,128)(2,1)S(1)} all-gather(bf16[128,256]{1,0:T(8,128)(2,1)S(1)} %get-tuple-element.35), channel_id=1, replica_groups=mesh['leaf'=4,'row'=16,'col'=8] {'col'}, dimensions={1}, use_global_device_ids=true | all-gather | bytes 589824 | tf_op jit(solution)/shard_map/all_gather | solution.py:121
  315.5 1.3 maximum_bitcast_fusion.2
  316.9 3.6 pad_maximum_fusion
  320.5 17.2 %all-gather.9.cloned.1.call-done = bf16[2,4096,256]{2,1,0:T(8,128)(2,1)} async-done(((bf16[2,256,256]{2,1,0:T(8,128)(2,1)}), bf16[2,4096,256]{2,1,0:T(8,128)(2,1)}) %all-gather.9.cloned.1.call-update) | async-done | bytes 4194320 | tf_op jit(solution)/shard_map/all_gather | solution.py:162
  337.7 39.1 %scatter_custom_fusion = bf16[12288,256]{1,0:T(8,128)(2,1)} fusion(s32[8192]{0:T(1024)S(1)} %bitcast.199, bf16[8192,256]{1,0:T(8,128)(2,1)} %bitcast.200, bf16[]{:T(256)} %constant.73.clone.1), kind=kCustom, calls=%fused_computation.3 | custom fusion | bytes 6291968
  376.8 7.6 %fusion.5 = bf16[2,384,256]{1,2,0:T(8,128)(2,1)S(1)} fusion(bf16[2,6144,256]{2,1,0:T(8,128)(2,1)} %bitcast.185, bf16[384,6144,1]{1,0,2:T(8,128)(2,1)} %bitcast.187, pred[2,384]{1,0:T(4,128)(4,1)S(1)} %compare_reduce_fusion), kind=kOutput, calls=%fused_computation.15 | convolution fusion | flops 2416508928 | bytes 11404032 | tf_op jit(solution)/shard_map/ab,ebn->ean/dot_general | solution.py:168
  385.4 55.5 %all-gather.11.cloned.1.call-done = bf16[2,3,128,2048]{3,2,1,0:T(8,128)(2,1)} async-done(((bf16[2,3,128,256]{3,2,1,0:T(8,128)(2,1)}), bf16[2,3,128,2048]{3,2,1,0:T(8,128)(2,1)}) %all-gather.11.cloned.1.call-update) | async-done | bytes 3145744 | tf_op jit(solution)/shard_map/all_gather | solution.py:176
  440.9 3.3 bitcast_convert_fusion
  444.2 3.8 copy.84
  448.0 3.4 copy.90
  453.0 60.0 %reduce-scatter.10.cloned.1.call-done = bf16[128,512]{1,0:T(8,128)(2,1)} async-done(((bf16[2048,512]{1,0:T(8,128)(2,1)}), bf16[128,512]{1,0:T(8,128)(2,1)}) %reduce-scatter.10.cloned.1.call-update) | async-done | bytes 131088
  (108 shorter events, 29.5 us)
Async XLA Ops:
  7.2 65.9 %copy-start.5 = (bf16[1,2,128,256]{3,2,1,0:T(8,128)(2,1)S(1)}, bf16[1,2,128,256]{3,2,1,0:T(8,128)(2,1)}, u32[]{:S(2)}) copy-start(bf16[1,2,128,256]{3,2,1,0:T(8,128)(2,1)} %param.14) | copy-start | bytes 393220
  7.2 121.0 %reduce-scatter.6.cloned.1.call-start = ((), (), s32[]{:S(2)}) async-start(), calls=%async_computation.5 | async-start | bytes 557056 | tf_op jit(solution)/shard_map/reduce_scatter | solution.py:81
  37.7 37.1 %copy-start.4 = (bf16[128,128]{1,0:T(8,128)(2,1)}, bf16[128,128]{1,0:T(8,128)(2,1)S(1)}, u32[]{:S(2)}) copy-start(bf16[128,128]{1,0:T(8,128)(2,1)S(1)} %fusion.7) | copy-start | bytes 98308
  62.7 15.7 %copy-start.8 = (bf16[1,128,128]{2,1,0:T(8,128)(2,1)S(1)}, bf16[1,128,128]{2,1,0:T(8,128)(2,1)}, u32[]{:S(2)}) copy-start(bf16[1,128,128]{2,1,0:T(8,128)(2,1)} %param.13) | copy-start | bytes 98308
  62.7 8.4 %collective-permute-start = (bf16[128,1024]{1,0:T(8,128)(2,1)S(1)}, bf16[128,1024]{1,0:T(8,128)(2,1)S(1)}, u32[]{:S(2)}, u32[]{:S(2)}) collective-permute-start(bf16[128,1024]{1,0:T(8,128)(2,1)S(1)} %all_gather.25), channel_id=1, source_target_pairs={{0,128},{128,0},{256,384},{384,256},{1,129},{129,1},{257,385},{385... | collective-permute-start | bytes 786440 | tf_op jit(solution)/shard_map/ppermute | solution.py:17
  72.4 100.4 %all-gather.5.cloned.1.call-start = ((), (), s32[]{:S(2)}) async-start(), calls=%async_computation.6 | async-start | bytes 2228224 | tf_op jit(solution)/shard_map/all_gather | solution.py:108
  74.8 80.9 %all-to-all-start = ((bf16[128,16,128]{2,0,1:T(8,128)(2,1)}), bf16[128,16,128]{2,0,1:T(8,128)(2,1)S(1)}, u32[]{:S(2)}, u32[]{:S(2)}) async-start(bf16[128,16,128]{2,0,1:T(8,128)(2,1)} %maximum_select_fusion.1), calls=%async_computation.1 | async-start | bytes 1048576 | tf_op jit(solution)/shard_map/all_to_all | solution.py:97
  78.4 138.1 %all-gather.7.cloned.1.call-start = ((), (), s32[]{:S(2)}) async-start(), calls=%async_computation.7 | async-start | bytes 1179648 | tf_op jit(solution)/shard_map/all_gather | solution.py:111
  153.0 8.4 %collective-permute-start.1 = (bf16[128,1024]{1,0:T(8,128)(2,1)S(1)}, bf16[128,1024]{1,0:T(8,128)(2,1)}, u32[]{:S(2)}, u32[]{:S(2)}) collective-permute-start(bf16[128,1024]{1,0:T(8,128)(2,1)S(1)} %all_gather.26), channel_id=1, source_target_pairs={{0,128},{128,0},{256,384},{384,256},{1,129},{129,1},{257,385},{385... | collective-permute-start | bytes 786440 | tf_op jit(solution)/shard_map/ppermute | solution.py:17
  162.5 1.6 copy-start.1
  164.1 52.4 %copy-start.2 = (bf16[2,128,256]{2,1,0:T(8,128)(2,1)S(1)}, bf16[2,128,256]{2,1,0:T(8,128)(2,1)}, u32[]{:S(2)}) copy-start(bf16[2,128,256]{2,1,0:T(8,128)(2,1)} %bitcast_select_fusion) | copy-start | bytes 393220
  172.8 46.6 %copy-start.12 = (s32[15]{0:T(128)S(1)}, s32[15]{0:T(128)}, u32[]{:S(2)}) copy-start(s32[15]{0:T(128)} %param.9) | copy-start | bytes 184
  172.8 46.9 %copy-start.3 = (bf16[2,256,256]{2,1,0:T(8,128)(2,1)S(1)}, bf16[2,256,256]{2,1,0:T(8,128)(2,1)}, u32[]{:S(2)}) copy-start(bf16[2,256,256]{2,1,0:T(8,128)(2,1)} %param.16) | copy-start | bytes 786436
  176.5 44.0 %copy-start.9 = (s32[2,32]{1,0:T(2,128)S(1)}, s32[2,32]{1,0:T(2,128)}, u32[]{:S(2)}) copy-start(s32[2,32]{1,0:T(2,128)} %param.10) | copy-start | bytes 772
  176.5 44.2 %copy-start.11 = (s32[2]{0:T(128)S(1)}, s32[2]{0:T(128)}, u32[]{:S(2)}) copy-start(s32[2]{0:T(128)} %constant.94) | copy-start | bytes 28
  176.5 44.3 %copy-start.10 = (s32[2]{0:T(128)S(1)}, s32[2]{0:T(128)}, u32[]{:S(2)}) copy-start(s32[2]{0:T(128)} %constant.97) | copy-start | bytes 28
  176.5 110.6 %reduce-scatter.8.cloned.1.call-start = ((), (), s32[]{:S(2)}) async-start(), calls=%async_computation.8 | async-start | bytes 1114112 | tf_op jit(solution)/shard_map/reduce_scatter | solution.py:113
  216.5 4.4 copy-start
  219.3 19.4 %copy-start.7 = (bf16[1,256,128]{2,1,0:T(8,128)(2,1)S(1)}, bf16[1,256,128]{2,1,0:T(8,128)(2,1)}, u32[]{:S(2)}) copy-start(bf16[1,256,128]{2,1,0:T(8,128)(2,1)} %param.15) | copy-start | bytes 196612
  219.4 118.3 %all-gather.9.cloned.1.call-start = ((), (), s32[]{:S(2)}) async-start(), calls=%async_computation.9 | async-start | bytes 4456448 | tf_op jit(solution)/shard_map/all_gather | solution.py:162
  231.1 36.4 %all-to-all-start.1 = ((bf16[16,2,128,128]{3,2,1,0:T(8,128)(2,1)}), bf16[16,2,128,128]{3,2,1,0:T(8,128)(2,1)}, u32[]{:S(2)}, u32[]{:S(2)}) async-start(bf16[16,2,128,128]{3,2,1,0:T(8,128)(2,1)} %fusion.9), calls=%async_computation.3 | async-start | bytes 2097152 | tf_op jit(solution)/shard_map/all_to_all | solution.py:125
  238.7 202.2 %all-gather.11.cloned.1.call-start = ((), (), s32[]{:S(2)}) async-start(), calls=%async_computation.10 | async-start | bytes 3538944 | tf_op jit(solution)/shard_map/all_gather | solution.py:176
  385.3 127.6 %reduce-scatter.10.cloned.1.call-start = ((), (), s32[]{:S(2)}) async-start(), calls=%async_computation.11 | async-start | bytes 2228224
  448.0 66.0 %copy-start.6 = (bf16[2,256,128]{2,1,0:T(8,128)(2,1)S(1)}, bf16[2,256,128]{2,1,0:T(8,128)(2,1)}, u32[]{:S(2)}) copy-start(bf16[2,256,128]{2,1,0:T(8,128)(2,1)} %param.17) | copy-start | bytes 393220
Sparse Core Ops, SparseCore 0:
  72.5 55.5 reduce-scatter.5
  131.1 41.6 all-gather.4
  176.6 39.8 all-gather.6
  219.5 67.5 reduce-scatter.7
  289.7 47.9 all-gather.8
  385.4 55.3 all-gather.10
  451.6 61.3 reduce-scatter.9
